TPU v7x, 32 devices: a whole 2x2x4 slice. The times are simulated.
32 devices in a mesh: site: 4 (over y, x), chan: 4 (over z), grp: 2 (over core).
Axes of the slice: x: 2, y: 2, z: 4, core: 2. Of those that a mesh axis runs over, the one named last changes fastest.
Arguments:
- voltages: bfloat16 [2, 8192, 3072], P(None, 'chan', ('site', 'grp')), may hold values from -6 to 6
- taps: float32 [8, 4], replicated, may hold values from -1 to 1
- sections: int32 [4, 2], replicated, may hold values from 0 to 768, as said below
- tile_list: int32 [2, 68, 2], replicated, may hold values from 0 to 15, as said below
Outputs:
- visibility: float32 [4, 4, 136, 2, 128, 128], P('site', 'chan', 'grp')
Inputs may be any that keep to these rules, and one draw needn't show every extreme that they name: `sections`: the live counts sum to 2048; each is at least 128 and at most 768, one site has exactly 768; each first live column plus its count is at most 768. `tile_list`: every pair (p, q) with 0 <= p <= q < 16 stands exactly once in the whole list.
All inputs are finite; a program needn't handle non-finite values.
Results may differ from a plain program's by a relative error of at most 0.0033.
Values may be sent and summed in bfloat16 or wider, within the bound.
A program may use at most 128 MiB of HBM per device.

v0:
```python
import jax
import jax.numpy as jnp
from jax import lax
from jax.sharding import PartitionSpec as P

NIN = 2048
PANEL = 128


slots_per_turn = 8


def from_behind(value, axis, steps):
    count = lax.axis_size(axis)
    leading, last = (max(0, -steps), min(count, count - steps))
    return lax.ppermute(value, axis, [(source, source + steps) for source in range(leading, last)])


def dft_table(chan_count):
    positions = jnp.arange(chan_count, dtype=jnp.int32)
    products = positions[:, None] * positions[None, :] % chan_count
    phases = products.astype(jnp.float32) * (2.0 * jnp.pi / chan_count)
    cosine_part = jnp.cos(phases)
    sine_part = jnp.sin(phases)
    from_real = jnp.stack([cosine_part, -sine_part], axis=1)
    from_imag = jnp.stack([sine_part, cosine_part], axis=1)
    return jnp.stack([from_real, from_imag], axis=0)


def filter_frames(history, taps, transform, frames):
    tap_count = taps.shape[0]
    filtered = jnp.zeros(
        (history.shape[0], frames, history.shape[2], history.shape[3]), jnp.float32
    )
    for tap_index in range(tap_count):
        first_frame = tap_count - 1 - tap_index
        filtered = (
            filtered
            + taps[tap_index][None, None, :, None] * history[:, first_frame : first_frame + frames]
        )
    spectra = jnp.einsum("qfkr,qkpm->pmfr", filtered, transform, precision=lax.Precision.HIGHEST)
    return spectra.astype(jnp.bfloat16)


def compact_inputs(spectra, sections, half_cols):
    site_total = sections.shape[0]
    row_width = site_total * half_cols
    group_total = spectra.shape[3] // row_width
    section_cols = group_total * half_cols
    counts = sections[:, 0]
    starts = sections[:, 1]
    offsets = jnp.cumsum(counts) - counts
    lead = spectra.shape[:3]
    buffer = jnp.zeros(lead + (NIN + section_cols,), spectra.dtype)
    blank = jnp.zeros(lead + (section_cols,), spectra.dtype)
    for site_id in range(site_total):
        pieces = [
            spectra[
                ..., g * row_width + site_id * half_cols : g * row_width + (site_id + 1) * half_cols
            ]
            for g in range(group_total)
        ]
        padded = jnp.concatenate(pieces + [blank], axis=3)
        live = lax.dynamic_slice_in_dim(padded, starts[site_id], section_cols, 3)
        buffer = lax.dynamic_update_slice_in_dim(buffer, live, offsets[site_id], 3)
    return buffer[..., :NIN]


def correlate(compact, slot_pairs):
    chan_local = compact.shape[1]
    slot_total = slot_pairs.shape[0]
    turns = -(-slot_total // slots_per_turn)
    filler = jnp.broadcast_to(slot_pairs[:1], (turns * slots_per_turn - slot_total, 2))
    grouped = jnp.concatenate([slot_pairs, filler], axis=0).reshape(turns, slots_per_turn, 2)

    def one_turn(turn_pairs):
        values = []
        for slot_index in range(slots_per_turn):
            left_panel = lax.dynamic_slice_in_dim(
                compact, turn_pairs[slot_index, 0] * PANEL, PANEL, 3
            )
            right_panel = lax.dynamic_slice_in_dim(
                compact, turn_pairs[slot_index, 1] * PANEL, PANEL, 3
            )
            gram_block = jnp.einsum(
                "qcfu,rcfv->cqruv", left_panel, right_panel, preferred_element_type=jnp.float32
            )
            real_part = gram_block[:, 0, 0] + gram_block[:, 1, 1]
            imag_part = gram_block[:, 1, 0] - gram_block[:, 0, 1]
            values.append(jnp.stack([real_part, imag_part], axis=1))
        return jnp.stack(values, axis=0)

    tile_values = lax.map(one_turn, grouped)
    tile_values = tile_values.reshape(turns * slots_per_turn, chan_local, 2, PANEL, PANEL)[
        :slot_total
    ]
    return jnp.moveaxis(tile_values, 0, 1)


def per_device(voltages, taps, sections, tile_list):
    tap_count, chan_count = taps.shape
    local_frames = voltages.shape[1] // chan_count
    half_cols = voltages.shape[2]
    signal = voltages.reshape(2, local_frames, chan_count, half_cols)
    last_frames = signal[:, local_frames - (tap_count - 1) :]
    earlier = from_behind(last_frames, "chan", 1)
    history = jnp.concatenate([earlier, signal], axis=1).astype(jnp.float32)
    spectra = filter_frames(history, taps, dft_table(chan_count), local_frames)
    blocked = lax.all_to_all(
        lax.all_to_all(spectra, "chan", split_axis=1, concat_axis=2, tiled=True),
        "site",
        split_axis=2,
        concat_axis=3,
        tiled=True,
    )
    gathered = lax.all_gather(blocked, "grp", axis=3, tiled=True)
    own_pairs = lax.dynamic_index_in_dim(tile_list, lax.axis_index("grp"), 0, keepdims=False)
    tile_values = correlate(compact_inputs(gathered, sections, half_cols), own_pairs)
    block_frames = gathered.shape[2]
    return (tile_values / block_frames)[None]


def solution(mesh):
    in_specs = (P(None, "chan", ("site", "grp")), P(), P(), P())
    out_specs = P("site", "chan", "grp", None, None, None)
    return jax.shard_map(
        per_device, mesh=mesh, in_specs=in_specs, out_specs=out_specs, check_vma=False
    )
```

profile of v0, /device:TPU:13, one launch (start us, length us, event | category | flops | bytes accessed | tf_op | source)
XLA Modules:
  0.0 524.5 jit_solution(8484824516320472824)
XLA Ops:
  6.5 4.9 reshape.607
  11.5 3.2 collective-permute-start
  16.2 1.4 maximum_convert_fusion
  17.6 22.3 %bitcast_convert_fusion = bf16[2,4,512,384]{3,1,2,0:T(4,128)(2,1)S(1)} fusion(f32[2,519,4,384]{3,2,0,1:T(4,128)S(1)} %maximum_convert_fusion, f32[4]{0:T(128)S(1)} %get-tuple-element.46, f32[4]{0:T(128)S(1)} %get-tuple-element.47, f32[4]{0:T(128)S(1)} %get-tuple-element.41, f32[4]{0:T(128)S(1)} %get-tuple-element.42, f32[4]{0:T(128)S(1)} %get-tuple-element.43, ...), kind=kOutput, calls=%fused_computation.119 | convolution fusion | flops 176160832 | bytes 53489664 | tf_op jit(solution)/shard_map/qfkr,qkpm->pmfr/dot_general | solution.py:41
  40.3 72.3 %all_to_all.30 = bf16[2,4,512,384]{3,2,0,1:T(8,128)(2,1)S(1)} all-to-all(bf16[2,4,512,384]{3,2,0,1:T(8,128)(2,1)S(1)} %copy.105), channel_id=1, replica_groups=mesh['site'=4,'chan'=4,'grp'=2] {'chan'}, dimensions={1} | all-to-all | bytes 6291456 | tf_op jit(solution)/shard_map/all_to_all | solution.py:110
  112.9 30.1 %copy.107 = bf16[2,1,2048,384]{3,0,1,2:T(2,128)(2,1)S(1)} copy(bf16[2,1,2048,384]{3,2,0,1:T(8,128)(2,1)S(1)} %bitcast.375) | data formatting | bytes 6291456 | tf_op jit(solution)/shard_map/all_to_all | solution.py:110
  143.0 36.7 %all_to_all.31 = bf16[2,1,2048,384]{3,0,1,2:T(2,128)(2,1)S(1)} all-to-all(bf16[2,1,2048,384]{3,0,1,2:T(2,128)(2,1)S(1)} %copy.107), channel_id=1, replica_groups=mesh['site'=4,'chan'=4,'grp'=2] {'site'}, dimensions={2} | all-to-all | bytes 6291456 | tf_op jit(solution)/shard_map/all_to_all | solution.py:109
  180.2 2.9 copy.109
  200.5 3.1 all-gather.2.cloned.1.call-done
  203.5 4.9 fusion.110
  208.4 2.3 copy.116
  210.7 2.3 copy.117
  213.0 2.3 copy.114
  215.3 2.3 copy.115
  222.3 2.5 fusion.93
  224.7 2.6 fusion.95
  227.4 3.7 fusion.97
  231.1 2.4 fusion.99
  233.5 2.9 broadcast_in_dim.26
  236.4 15.0 %dynamic_update_slice.16 = bf16[2,1,512,2816]{3,2,0,1:T(8,128)(2,1)} dynamic-update-slice(bf16[2,1,512,2816]{3,2,0,1:T(8,128)(2,1)} %broadcast_in_dim.26, bf16[2,1,512,768]{3,2,0,1:T(8,128)(2,1)} %fusion.99, s32[]{:T(128)} %constant.61.clone.1, s32[]{:T(128)} %constant.61.clone.1, s32[]{:T(128)} %constant.61.clone.1, s32[]{:T(128)S(6)} %select_n.107) | dynamic-update-slice | bytes 3145732 | tf_op jit(solution)/shard_map/dynamic_update_slice | solution.py:65
  251.4 15.0 %dynamic_update_slice.17 = bf16[2,1,512,2816]{3,2,0,1:T(8,128)(2,1)} dynamic-update-slice(bf16[2,1,512,2816]{3,2,0,1:T(8,128)(2,1)} %dynamic_update_slice.16, bf16[2,1,512,768]{3,2,0,1:T(8,128)(2,1)} %fusion.97, s32[]{:T(128)} %constant.61.clone.1, s32[]{:T(128)} %constant.61.clone.1, s32[]{:T(128)} %constant.61.clone.1, s32[]{:T(128)S(6)} %select_n.109) | dynamic-update-slice | bytes 3145732 | tf_op jit(solution)/shard_map/dynamic_update_slice | solution.py:65
  266.5 16.1 %dynamic_update_slice.18 = bf16[2,1,512,2816]{3,2,0,1:T(8,128)(2,1)} dynamic-update-slice(bf16[2,1,512,2816]{3,2,0,1:T(8,128)(2,1)} %dynamic_update_slice.17, bf16[2,1,512,768]{3,2,0,1:T(8,128)(2,1)S(1)} %fusion.95, s32[]{:T(128)} %constant.61.clone.1, s32[]{:T(128)} %constant.61.clone.1, s32[]{:T(128)} %constant.61.clone.1, s32[]{:T(128)S(6)} %select_n.111) | dynamic-update-slice | bytes 3145732 | tf_op jit(solution)/shard_map/dynamic_update_slice | solution.py:65
  282.6 16.1 %dynamic_update_slice.19 = bf16[2,1,512,2816]{3,2,0,1:T(8,128)(2,1)} dynamic-update-slice(bf16[2,1,512,2816]{3,2,0,1:T(8,128)(2,1)} %dynamic_update_slice.18, bf16[2,1,512,768]{3,2,0,1:T(8,128)(2,1)S(1)} %fusion.93, s32[]{:T(128)} %constant.61.clone.1, s32[]{:T(128)} %constant.61.clone.1, s32[]{:T(128)} %constant.61.clone.1, s32[]{:T(128)S(6)} %select_n.113) | dynamic-update-slice | bytes 3145732 | tf_op jit(solution)/shard_map/dynamic_update_slice | solution.py:65
  298.7 4.8 slice.355
  303.5 205.2 %while.10 = (s32[]{:T(128)}, f32[9,8,1,2,128,128]{5,4,3,1,0,2:T(8,128)}, s32[9,8,2]{1,0,2:T(8,128)S(1)}, bf16[2,1,512,2048]{3,2,0,1:T(8,128)(2,1)}, s32[]{:T(128)}, /*index=5*/s32[1,1]{0,1:T(1,128)}, s32[]{:T(128)}, s32[]{:T(128)}) while((s32[]{:T(128)}, f32[9,8,1,2,128,128]{5,4,3,1,0,2:T(8,128)}, s32[9,8,2]{1,0,2:T(8,128)S(1)}, ...), condition=%wide.region_2.3_spmd, body=%wide.region_1.2_spmd.sunk | while | flops 537395200 | bytes 15730297 | solution.py:93
  308.0 1.3 convolution_bitcast_fusion.17
  320.9 1.4 convolution_bitcast_fusion.22
  333.5 1.3 convolution_bitcast_fusion.18
  338.7 1.3 convolution_bitcast_fusion.20
  356.3 1.3 convolution_bitcast_fusion.18
  364.1 1.3 convolution_bitcast_fusion.21
  366.6 1.3 convolution_bitcast_fusion.22
  376.4 1.3 convolution_bitcast_fusion.17
  379.1 1.3 convolution_bitcast_fusion.18
  399.2 1.3 convolution_bitcast_fusion.17
  401.9 1.3 convolution_bitcast_fusion.18
  409.7 1.3 convolution_bitcast_fusion.21
  412.1 1.3 convolution_bitcast_fusion.22
  422.0 1.3 convolution_bitcast_fusion.17
  427.2 1.3 convolution_bitcast_fusion.19
  429.9 1.3 convolution_bitcast_fusion.20
  452.7 1.3 convolution_bitcast_fusion.20
  457.7 1.3 convolution_bitcast_fusion.22
  478.0 1.3 convolution_bitcast_fusion.21
  487.8 1.3 convolution_bitcast_fusion.16
  490.4 1.3 convolution_bitcast_fusion.17
  503.3 1.3 convolution_bitcast_fusion.22
  508.7 8.9 %fusion.65 = f32[1,1,68,2,128,128]{5,4,3,2,1,0:T(8,128)} fusion(f32[72,1,2,128,128]{4,3,2,0,1:T(8,128)} %bitcast.377), kind=kLoop, calls=%fused_computation.101 | loop fusion | flops 2228224 | bytes 17825792 | tf_op jit(solution)/shard_map/div | solution.py:120
  (286 shorter events, 96.0 us)
Async XLA Ops:
  6.5 188.3 %copy-start = (s32[2,68,2]{1,2,0:T(2,128)S(1)}, s32[2,68,2]{1,2,0:T(2,128)}, u32[]{:S(2)}) copy-start(s32[2,68,2]{1,2,0:T(2,128)} %param.9) | copy-start | bytes 3268
  6.5 8.3 %copy-start.5 = (f32[8,4]{0,1:T(4,128)S(1)}, f32[8,4]{0,1:T(4,128)}, u32[]{:S(2)}) copy-start(f32[8,4]{0,1:T(4,128)} %param.7) | copy-start | bytes 388
  6.5 197.0 %all-gather.2.cloned.1.call-start = ((), (), s32[]{:S(2)}) async-start(), calls=%async_computation.2 | async-start | bytes 9437184 | tf_op jit(solution)/shard_map/all_gather | solution.py:116
  11.5 4.8 collective-permute-start
  180.1 2.9 copy-start.6
  180.2 8.5 %slice-start = ((s32[4,2]{0,1:T(2,128)}), s32[4,1]{0,1:T(1,128)S(1)}, s32[]{:S(2)}) async-start(s32[4,2]{0,1:T(2,128)} %param.8), calls=%async_computation.3 | async-start | bytes 1024 | tf_op jit(solution)/shard_map/slice | solution.py:50
  218.8 3.5 copy-start.4
  222.3 8.9 %copy-start.2 = (bf16[2,1,512,384]{3,2,0,1:T(8,128)(2,1)S(1)}, bf16[2,1,512,384]{3,2,0,1:T(8,128)(2,1)}, u32[]{:S(2)}) copy-start(bf16[2,1,512,384]{3,2,0,1:T(8,128)(2,1)} %copy.110) | copy-start | bytes 2359300
  222.3 8.9 %copy-start.3 = (bf16[2,1,512,384]{3,2,0,1:T(8,128)(2,1)S(1)}, bf16[2,1,512,384]{3,2,0,1:T(8,128)(2,1)}, u32[]{:S(2)}) copy-start(bf16[2,1,512,384]{3,2,0,1:T(8,128)(2,1)} %copy.111) | copy-start | bytes 2359300
  508.7 8.9 %copy-start.1 = (s32[2,68,2]{1,2,0:T(2,128)S(1)}, s32[2,68,2]{1,2,0:T(2,128)}, u32[]{:S(2)}) copy-start(s32[2,68,2]{1,2,0:T(2,128)} %param.9) | copy-start | bytes 3268
Sparse Core Ops, SparseCore 0:
  183.2 20.2 all-gather.1
where the time goes:
time: 533 us; the launch traced here: 525 us
  local copies, waits for them, and re-layouts  149 us (28%)
  matrix products  116 us (22%)
  blocking collectives  109 us (20%)
  loops' own time  89.7 us (17%)
  between operations  28.9 us (5%)
  other arithmetic  23.9 us (4%)
    dot_general x72, matrix products, one_turn(): jnp.einsum('qcfu,rcfv->cqruv', left_panel, right_panel, preferred_element...  94.2 us
    another operation x1, loops' own time, correlate(): tile_values = lax.map(one_turn, grouped)  89.7 us
    all_to_all x1, blocking collectives, per_device(): lax.all_to_all(spectra, 'chan', split_axis=1, concat_axis=2, tiled=True)  72.3 us
    dynamic_update_slice x4, local copies, waits for them, and re-layouts, compact_inputs(): buffer = lax.dynamic_update_slice_in_dim(buffer, live, offsets[site_id], 3)  62.3 us
    all_to_all x1, blocking collectives, per_device(): lax.all_to_all(lax.all_to_all(spectra, 'chan', split_axis=1, concat_axis=...  36.7 us
    all_to_all x2, local copies, waits for them, and re-layouts, per_device(): lax.all_to_all(spectra, 'chan', split_axis=1, concat_axis=2, tiled=True)  30.4 us
    dot_general x1, matrix products, filter_frames(): jnp.einsum('qfkr,qkpm->pmfr', filtered, transform, precision=lax.Precisio...  22.3 us
    slice x9, local copies, waits for them, and re-layouts, compact_inputs(): spectra[..., g * row_width + site_id * half_cols:g * row_width + (site_id...  18.7 us
  transfers between devices with their start and end apart: 2, of which 2 were waited for; matrix products, arithmetic and copies ran while one was open for 1% of the time, Pallas kernels for 0%

commit v1 on v0

v1 whole, which is shorter than its diff:
```python
import functools

import jax
import jax.numpy as jnp
import numpy as np
from jax import lax
from jax.experimental import pallas as pl
from jax.experimental.pallas import tpu as pltpu
from jax.sharding import PartitionSpec as P

NIN = 2048
PANEL = 128
CHUNKS = 4
MESH = pl.DeviceIdType.MESH


def filter_constants(tap_count, chan_count, frames):
    width = (tap_count + frames) * chan_count
    sample = np.arange(width)
    position = sample % chan_count
    pos = np.stack([sample // chan_count, position]).astype(np.int32)
    chan = np.arange(chan_count)
    phase = (chan[:, None] * position[None, :] % chan_count) * (2.0 * np.pi / chan_count)
    cosine, sine = np.cos(phase), np.sin(phase)
    table = np.stack([np.stack([cosine, sine], 1), np.stack([-sine, cosine], 1)], 1)
    return pos, table.reshape(chan_count * 4, width).astype(np.float32)


def exchange_kernel(
    dims, x_ref, taps_ref, pos_ref, table_ref, out_ref,
    spec_ref, land_ref, halo_ref, weight_ref,
    halo_sem, z_send, z_recv, x_send, x_recv, g_send, g_recv,
):
    tap_count, chan_count, frames, sub, n_site, n_chan, n_grp = dims
    cols = x_ref.shape[2]
    ratio = n_chan // n_site
    chunk = frames // CHUNKS
    width = (tap_count + sub) * chan_count
    back = tap_count * chan_count
    site, chan, grp = lax.axis_index("site"), lax.axis_index("chan"), lax.axis_index("grp")

    def offset(me, step, total):
        return lax.rem(me + step, total)

    barrier = pltpu.get_barrier_semaphore()
    partners = 0
    for name, me, total in (("chan", chan, n_chan), ("site", site, n_site), ("grp", grp, n_grp)):
        for step in range(1, total):
            pl.semaphore_signal(
                barrier, inc=1, device_id={name: offset(me, step, total)}, device_id_type=MESH
            )
            partners += 1
    pl.semaphore_wait(barrier, partners)

    def halo_copy():
        return pltpu.make_async_remote_copy(
            src_ref=x_ref.at[:, pl.ds(x_ref.shape[1] - back, back), :],
            dst_ref=halo_ref,
            send_sem=halo_sem.at[0],
            recv_sem=halo_sem.at[1],
            device_id={"chan": offset(chan, 1, n_chan)},
            device_id_type=MESH,
        )

    @pl.when(chan < n_chan - 1)
    def _():
        halo_copy().start()

    frame_of = pos_ref[0:1, :]
    place_of = pos_ref[1:2, :]
    lag = lax.broadcasted_iota(jnp.int32, (sub, width), 0) + tap_count - frame_of
    base = jnp.zeros((sub, width), jnp.float32)
    for t in range(tap_count):
        row = jnp.zeros((1, width), jnp.float32)
        for k in range(chan_count):
            row = jnp.where(place_of == k, taps_ref[t, k], row)
        base = jnp.where(lag == t, row, base)
    for m in range(chan_count):
        for q in range(2):
            for p in range(2):
                index = (m * 2 + q) * 2 + p
                full = base * table_ref[index : index + 1, :]
                high = full.astype(jnp.bfloat16)
                low = (full - high.astype(jnp.float32)).astype(jnp.bfloat16)
                rows = pl.ds((m * 2 + q) * sub, sub)
                weight_ref[p, 0, rows, :] = high
                weight_ref[p, 1, rows, :] = low

    def put_spectra(first_frame, window):
        total = None
        for p in range(2):
            for part in range(2):
                term = jnp.dot(
                    weight_ref[p, part], window[p], preferred_element_type=jnp.float32
                )
                total = term if total is None else total + term
        total = total.astype(jnp.bfloat16).reshape(chan_count, 2, sub, cols)
        spec_ref[:, :, pl.ds(pl.multiple_of(first_frame, 16), sub), :] = total

    def filter_chunk(k):
        per_chunk = chunk // sub
        if k == 0:
            @pl.when(chan == 0)
            def _():
                halo_ref[...] = jnp.zeros_like(halo_ref)

            @pl.when(chan > 0)
            def _():
                halo_copy().wait_recv()

            put_spectra(
                0,
                [
                    jnp.concatenate([halo_ref[p], x_ref[p, : sub * chan_count, :]], axis=0)
                    for p in range(2)
                ],
            )

        def body(u, carry):
            first = (k * per_chunk + u) * sub
            start = pl.multiple_of(first * chan_count - back, 16)
            put_spectra(first, [x_ref[p, pl.ds(start, width), :] for p in range(2)])
            return carry

        lax.fori_loop(1 if k == 0 else 0, per_chunk, body, 0)

    def span(k):
        return pl.ds(k * chunk, chunk)

    def z_copy(step, k):
        there = offset(chan, step, n_chan)
        return pltpu.make_async_remote_copy(
            src_ref=spec_ref.at[there, :, span(k), :],
            dst_ref=land_ref.at[chan, :, span(k), :],
            send_sem=z_send.at[step, k],
            recv_sem=z_recv.at[step, k],
            device_id={"chan": there},
            device_id_type=MESH,
        )

    def slot(section, sub_block, k):
        start = pl.multiple_of(sub_block * frames + k * chunk, 16)
        return out_ref.at[section, :, pl.ds(start, chunk), :]

    def forward(step, k, own, begin):
        block = lax.rem(chan + n_chan - step, n_chan)
        owner = block // ratio
        sub_block = lax.rem(block, ratio)
        source = spec_ref.at[chan, :, span(k), :] if own else land_ref.at[block, :, span(k), :]
        target = slot(site * n_grp + grp, sub_block, k)

        @pl.when(owner != site)
        def _():
            copy = pltpu.make_async_remote_copy(
                src_ref=source,
                dst_ref=target,
                send_sem=x_send.at[step, k],
                recv_sem=x_recv.at[site, sub_block, k],
                device_id={"site": owner},
                device_id_type=MESH,
            )
            if begin:
                copy.start()
            else:
                copy.wait_send()

        if begin:
            @pl.when(owner == site)
            def _():
                pltpu.make_async_copy(source, target, x_recv.at[site, sub_block, k]).start()

    def cross(from_site, sub_block, k):
        mine = slot(from_site * n_grp + grp, sub_block, k)
        return [
            pltpu.make_async_remote_copy(
                src_ref=mine,
                dst_ref=mine,
                send_sem=g_send.at[step - 1, from_site, sub_block, k],
                recv_sem=g_recv.at[step - 1, from_site, sub_block, k],
                device_id={"grp": offset(grp, step, n_grp)},
                device_id_type=MESH,
            )
            for step in range(1, n_grp)
        ]

    def each(body, *sizes):
        low, high = sizes
        def run(index, carry):
            body(index)
            return carry
        lax.fori_loop(low, high, run, 0, unroll=high - low <= 4)

    def over_blocks(body):
        def run(index):
            body(lax.rem(index // ratio + site, n_site), lax.rem(index, ratio))
        each(run, 0, n_site * ratio)

    order = list(range(1, CHUNKS)) + [0]
    for k in order:
        filter_chunk(k)
        each(lambda step: z_copy(step, k).start(), 1, n_chan)
        forward(0, k, True, True)

    def hand_over(k):
        def run(from_site, sub_block):
            here = slot(from_site * n_grp + grp, sub_block, k)
            pltpu.make_async_copy(here, here, x_recv.at[from_site, sub_block, k]).wait()
            for copy in cross(from_site, sub_block, k):
                copy.start()
        over_blocks(run)

    for place, k in enumerate(order):
        def relay(step):
            z_copy(step, k).wait_recv()
            forward(step, k, False, True)
        each(relay, 1, n_chan)
        if place:
            hand_over(order[place - 1])
    hand_over(order[-1])

    @pl.when(chan < n_chan - 1)
    def _():
        halo_copy().wait_send()

    for k in order:
        each(lambda step: z_copy(step, k).wait_send(), 1, n_chan)
        forward(0, k, True, False)
        each(lambda step: forward(step, k, False, False), 1, n_chan)

        def finish(from_site, sub_block):
            for copy in cross(from_site, sub_block, k):
                copy.wait_send()
                copy.wait_recv()
        over_blocks(finish)


def exchange(voltages, taps):
    tap_count, chan_count = taps.shape
    n_site, n_chan, n_grp = (lax.axis_size(a) for a in ("site", "chan", "grp"))
    assert n_chan == chan_count
    frames = voltages.shape[1] // chan_count
    cols = voltages.shape[2]
    sub = min(frames // CHUNKS, max(16, 128 // chan_count))
    width = (tap_count + sub) * chan_count
    ratio = n_chan // n_site
    pos, table = filter_constants(tap_count, chan_count, sub)
    dims = (tap_count, chan_count, frames, sub, n_site, n_chan, n_grp)
    vmem = pl.BlockSpec(memory_space=pltpu.VMEM)
    dma = pltpu.SemaphoreType.DMA
    return pl.pallas_call(
        functools.partial(exchange_kernel, dims),
        out_shape=jax.ShapeDtypeStruct((n_site * n_grp, 2, ratio * frames, cols), jnp.bfloat16),
        in_specs=[vmem, pl.BlockSpec(memory_space=pltpu.SMEM), vmem, vmem],
        out_specs=pl.BlockSpec(memory_space=pl.ANY),
        scratch_shapes=[
            pltpu.VMEM((chan_count, 2, frames, cols), jnp.bfloat16),
            pltpu.VMEM((n_chan, 2, frames, cols), jnp.bfloat16),
            pltpu.VMEM((2, tap_count * chan_count, cols), jnp.bfloat16),
            pltpu.VMEM((2, 2, chan_count * 2 * sub, width), jnp.bfloat16),
            dma((2,)),
            dma((n_chan, CHUNKS)),
            dma((n_chan, CHUNKS)),
            dma((n_chan, CHUNKS)),
            dma((n_site, ratio, CHUNKS)),
            dma((n_grp - 1, n_site, ratio, CHUNKS)),
            dma((n_grp - 1, n_site, ratio, CHUNKS)),
        ],
        compiler_params=pltpu.CompilerParams(
            collective_id=0, has_side_effects=True, vmem_limit_bytes=48 * 1024 * 1024
        ),
    )(voltages, taps, jnp.asarray(pos), jnp.asarray(table))


def tiles_kernel(dims, sections_ref, pairs_ref, spec_ref, out_ref, left_ref, right_ref):
    n_site, n_grp, per_step = dims
    frames, cols = spec_ref.shape[2:]
    per_half = cols // PANEL
    blocks = n_grp * per_half
    step = pl.program_id(0)

    @pl.when(step == 0)
    def _():
        counts = [sections_ref[s, 0] for s in range(n_site)]
        offsets = [jnp.int32(0)]
        for s in range(n_site - 1):
            offsets.append(offsets[-1] + counts[s])
        source = lax.broadcasted_iota(jnp.int32, (2 * PANEL, PANEL), 0)
        column = lax.broadcasted_iota(jnp.int32, (2 * PANEL, PANEL), 1)

        def one_panel(panel, carry):
            first = panel * PANEL

            def site_of(index):
                return sum((index >= offsets[s]).astype(jnp.int32) for s in range(1, n_site))

            low_site, high_site = site_of(first), site_of(first + PANEL - 1)
            windows, selects = [], []
            for which, owner in enumerate((low_site, high_site)):
                offset = sum(jnp.where(s < owner, counts[s], 0) for s in range(n_site - 1))
                count, start = sections_ref[owner, 0], sections_ref[owner, 1]
                begin = start - offset + first
                block = jnp.clip(begin >> (PANEL.bit_length() - 1), 0, blocks - 2)
                shift = begin - block * PANEL
                low = offset - first
                high = low + count
                if which:
                    high = jnp.where(low_site == high_site, low, high)
                hit = (source == column + shift) & (column >= low) & (column < high)
                selects.append(hit.astype(jnp.float32).astype(jnp.bfloat16))
                for extra in range(2):
                    here = block + extra
                    half = here // per_half
                    lane = pl.multiple_of((here - half * per_half) * PANEL, PANEL)
                    part = spec_ref[owner * n_grp + half, :, :, pl.ds(lane, PANEL)]
                    windows.append(part.reshape(2 * frames, PANEL))
            packed = jnp.dot(
                jnp.concatenate(windows, axis=1),
                jnp.concatenate(selects, axis=0),
                preferred_element_type=jnp.float32,
            )
            value = packed.astype(jnp.bfloat16)
            right_ref[panel, :, :PANEL] = value
            right_ref[panel, :frames, PANEL:] = -value[frames:]
            right_ref[panel, frames:, PANEL:] = value[:frames]
            left_ref[panel] = packed.T.astype(jnp.bfloat16)
            return carry

        lax.fori_loop(0, NIN // PANEL, one_panel, 0)

    slots = pl.num_programs(0) * per_step
    base = (lax.axis_index("grp") * slots + step * per_step) * 2
    for i in range(per_step):
        tile = jnp.dot(
            left_ref[pairs_ref[base + 2 * i]],
            right_ref[pairs_ref[base + 2 * i + 1]],
            preferred_element_type=jnp.float32,
        ) * (1.0 / frames)
        out_ref[0, 0, i, 0] = tile[:, :PANEL]
        out_ref[0, 0, i, 1] = tile[:, PANEL:]


def correlate(spectra, sections, tile_list):
    n_site, n_grp = lax.axis_size("site"), lax.axis_size("grp")
    slots = tile_list.shape[1]
    per_step = max(d for d in range(1, 5) if slots % d == 0)
    frames = spectra.shape[2]
    panels = NIN // PANEL
    return pl.pallas_call(
        functools.partial(tiles_kernel, (n_site, n_grp, per_step)),
        out_shape=jax.ShapeDtypeStruct((1, 1, slots, 2, PANEL, PANEL), jnp.float32),
        grid_spec=pltpu.PrefetchScalarGridSpec(
            num_scalar_prefetch=2,
            grid=(slots // per_step,),
            in_specs=[pl.BlockSpec(memory_space=pltpu.VMEM)],
            out_specs=pl.BlockSpec(
                (1, 1, per_step, 2, PANEL, PANEL), lambda i, *_: (0, 0, i, 0, 0, 0)
            ),
            scratch_shapes=[
                pltpu.VMEM((panels, PANEL, 2 * frames), jnp.bfloat16),
                pltpu.VMEM((panels, 2 * frames, 2 * PANEL), jnp.bfloat16),
            ],
        ),
        compiler_params=pltpu.CompilerParams(vmem_limit_bytes=48 * 1024 * 1024),
    )(sections, tile_list.reshape(-1), spectra)


def per_device(voltages, taps, sections, tile_list):
    return correlate(exchange(voltages, taps), sections, tile_list)


def solution(mesh):
    in_specs = (P(None, "chan", ("site", "grp")), P(), P(), P())
    out_specs = P("site", "chan", "grp", None, None, None)
    return jax.shard_map(
        per_device, mesh=mesh, in_specs=in_specs, out_specs=out_specs, check_vma=False
    )
```

time: 533 us -> 116 us (0.22); the launches traced: 525 us -> 115 us
  local copies, waits for them, and re-layouts: 149 us -> 5.74 us
  matrix products: 116 us -> 0 us
  Pallas kernels: 0 us -> 110 us
  blocking collectives: 109 us -> 0 us
  loops' own time: 89.7 us -> 0 us
  between operations: 28.9 us -> 0.02 us
  other arithmetic: 23.9 us -> 0 us
    dot_general x73 -> x0, matrix products: 116 us -> none  [the longest x72 94.2 us: one_turn(): jnp.einsum('qcfu,rcfv->cqruv', left_panel, right_panel, preferred_element...]
    pallas_call x0 -> x2, Pallas kernels: none -> 110 us  [the longest x1 86.5 us: exchange(): pl.pallas_call(functools.partial(exchange_kernel, dims), out_shape=jax.Sh...]
    all_to_all x2 -> x0, blocking collectives: 109 us -> none  [the longest x1 72.3 us: per_device(): lax.all_to_all(spectra, 'chan', split_axis=1, concat_axis=2, tiled=True)]
    another operation x1 -> x0, loops' own time: 89.7 us -> none  [correlate(): tile_values = lax.map(one_turn, grouped)]
    dynamic_update_slice x22 -> x0, local copies, waits for them, and re-layouts: 75 us -> none  [the longest x4 62.3 us: compact_inputs(): buffer = lax.dynamic_update_slice_in_dim(buffer, live, offsets[site_id], 3)]
    all_to_all x4 -> x0, local copies, waits for them, and re-layouts: 33.7 us -> none  [the longest x2 30.4 us: per_device(): lax.all_to_all(spectra, 'chan', split_axis=1, concat_axis=2, tiled=True)]
    slice x26 -> x0, local copies, waits for them, and re-layouts: 31.8 us -> none  [the longest x9 18.7 us: compact_inputs(): spectra[..., g * row_width + site_id * half_cols:g * row_width + (site_id...]
    concatenate x5 -> x0, other arithmetic: 11.3 us -> none  [the longest x4 11.2 us: compact_inputs(): padded = jnp.concatenate(pieces + [blank], axis=3)]
  transfers between devices with their start and end apart: 2 -> 0, of which waited for: 2 -> 0; matrix products, arithmetic and copies ran while one was open for 1% -> 0% of each run, Pallas kernels for 0% -> 0%
where the time goes in v1:
time: 116 us; the launch traced here: 115 us
  Pallas kernels  110 us (95%)
  local copies, waits for them, and re-layouts  5.74 us (5%)
    pallas_call x1, Pallas kernels, exchange(): pl.pallas_call(functools.partial(exchange_kernel, dims), out_shape=jax.Sh...  86.5 us
    pallas_call x1, Pallas kernels, correlate(): pl.pallas_call(functools.partial(tiles_kernel, (n_site, n_grp, per_step))...  23.2 us
    unnamed x9, local copies, waits for them, and re-layouts  5.6 us

profile of v1, /device:TPU:13, one launch (start us, length us, event | category | flops | bytes accessed | tf_op | source)
XLA Modules:
  0.0 115.5 jit_solution(11913610987700255023)
XLA Ops:
  0.0 0.8 copy.11.sections_ref
  0.8 0.8 copy.10.taps_ref
  1.5 0.8 copy.9
  2.3 0.1 reshape.3.pairs_ref
  2.5 0.0 copy-start
  2.5 1.9 %copy-done = bf16[2,2048,384]{2,1,0:T(8,128)(2,1)S(1)} copy-done((bf16[2,2048,384]{2,1,0:T(8,128)(2,1)S(1)}, bf16[2,2048,384]{2,1,0:T(8,128)(2,1)}, u32[]{:S(2)}) %copy-start) | copy-done | bytes 3145752
  4.4 0.0 copy-start.1
  4.4 0.7 copy-done.1
  5.1 0.0 copy-start.2
  5.1 0.7 copy-done.2
  5.8 86.5 %shard_map.64.spec_ref = bf16[8,2,512,384]{3,2,1,0:T(8,128)(2,1)} custom-call(bf16[2,2048,384]{2,1,0:T(8,128)(2,1)S(1)} %copy-done, f32[8,4]{1,0:T(8,128)S(1)} %copy.10.taps_ref, s32[2,160]{1,0:T(2,128)S(1)} %copy-done.2, f32[16,160]{1,0:T(8,128)S(1)} %copy-done.1), custom_call_target="tpu_custom_call" | custom-call | tf_op jit(solution)/shard_map/pallas_call | solution.py:250
  92.3 23.2 %shard_map.65 = f32[1,1,68,2,128,128]{5,4,3,2,1,0:T(8,128)} custom-call(s32[4,2]{1,0:T(4,128)S(1)} %copy.11.sections_ref, s32[272]{0:T(512)S(1)} %reshape.3.pairs_ref, bf16[8,2,512,384]{3,2,1,0:T(8,128)(2,1)} %shard_map.64.spec_ref), custom_call_target="tpu_custom_call" | custom-call | tf_op jit(solution)/shard_map/pallas_call | solution.py:348
Async XLA Ops:
  2.5 1.9 %copy-start = (bf16[2,2048,384]{2,1,0:T(8,128)(2,1)S(1)}, bf16[2,2048,384]{2,1,0:T(8,128)(2,1)}, u32[]{:S(2)}) copy-start(bf16[2,2048,384]{2,1,0:T(8,128)(2,1)} %x_ref.1) | copy-start | bytes 9437188
  4.4 0.7 copy-start.1
  5.1 0.7 copy-start.2
